TPU v7x, 512 devices: a whole 4x4x16 slice. The times are simulated.
512 devices in a mesh: lon: 64 (over y, z_lo, core), rad: 8 (over z_hi, x).
Axes of the slice: x: 4, y: 4, z: 16 (z_hi: 2, z_lo: 8; z = z_hi * 8 + z_lo), core: 2. Of those that a mesh axis runs over, the one named last changes fastest.
Arguments:
- logvisc: float32 [96, 256, 512], P('rad', 'lon'), may hold values from -1 to 1
- momentum: float32 [96, 256, 512], P('rad', 'lon'), may hold values from -6 to 6
- displacement: float32 [3, 96, 256, 512], P(None, 'rad', 'lon'), may hold values from -6 to 6
- ice_history: float32 [8, 256, 512], P(None, 'lon'), may hold values from -6 to 6
- load_steps: int32 [2], replicated, may hold values from 0 to 7
- site_cells: int32 [768], P('lon'), may hold values from 0 to 131071
- observed: float32 [3, 768], P(None, 'lon'), may hold values from -6 to 6
- site_weight: float32 [3, 768], P(None, 'lon'), may hold values from 2 to 6
Outputs:
- new_logvisc: float32 [96, 256, 512], P('rad', 'lon')
- half_momentum: float32 [96, 256, 512], P('rad', 'lon')
- misfit: float32 [1], replicated
Inputs may be any that keep to these rules, and one draw needn't show every extreme that they name: site_cells holds lon * 512 + lat of the surface cell where the site stands. load_steps indexes the first dimension of ice_history.
All inputs are finite; a program needn't handle non-finite values.
Results may differ from a plain program's by a relative error of at most 0.0003.
Values sent between devices are 32-bit elements; how exact they have to be, the bound alone decides.
A program may use at most 64 MiB of HBM per device.

v0:
```python
import math
import jax
import jax.numpy as jnp
from jax import lax
from jax.sharding import PartitionSpec as P

RELAX = 2
RELAX_RATE = 0.05
KERNEL_WIDTH = 0.1
KERNEL_WAVE = 40.0
PRIOR_WEIGHT = 0.1
LOAD_FACTOR = 1.0


def extended(block, sides, width, periodic):
    for axis, dim in sides:
        count = lax.axis_size(axis)
        forward = [(i, i + 1) for i in range(count - 1)]
        if periodic:
            forward.append((count - 1, 0))
        backward = [(target, source) for source, target in forward]
        low = lax.ppermute(
            lax.slice_in_dim(block, block.shape[dim] - width, None, axis=dim), axis, forward
        )
        high = lax.ppermute(lax.slice_in_dim(block, 0, width, axis=dim), axis, backward)
        block = jnp.concatenate([low, block, high], axis=dim)
    return block


def harmonic(center_fluid, other_fluid):
    summed = center_fluid + other_fluid
    coeff = 2.0 * center_fluid * other_fluid / summed
    slope = 2.0 * other_fluid * other_fluid / (summed * summed)
    return (coeff, slope)


def neighbours(padded):
    return [
        padded[:, 2:, 1:-1, 1:-1],
        padded[:, :-2, 1:-1, 1:-1],
        padded[:, 1:-1, 2:, 1:-1],
        padded[:, 1:-1, :-2, 1:-1],
        padded[:, 1:-1, 1:-1, 2:],
        padded[:, 1:-1, 1:-1, :-2],
    ]


def middle(padded):
    return padded[:, 1:-1, 1:-1, 1:-1]


def apply_operator(field_pad, fluid_pad):
    fluid_mid = middle(fluid_pad)
    field_mid = middle(field_pad)
    total = jnp.zeros(field_mid.shape, jnp.float32)
    for fluid_side, field_side in zip(neighbours(fluid_pad), neighbours(field_pad)):
        coeff, slope = harmonic(fluid_mid, fluid_side)
        total = total + coeff * (field_side - field_mid)
    return total


def fluid_gradient(state_pad, adjoint_pad, fluid_pad):
    fluid_mid = middle(fluid_pad)
    state_mid = middle(state_pad)
    adjoint_mid = middle(adjoint_pad)
    total = jnp.zeros(fluid_mid.shape, jnp.float32)
    for fluid_side, state_side, adjoint_side in zip(
        neighbours(fluid_pad), neighbours(state_pad), neighbours(adjoint_pad)
    ):
        coeff, slope = harmonic(fluid_mid, fluid_side)
        product = jnp.sum(
            (state_side - state_mid) * (adjoint_side - adjoint_mid), axis=0, keepdims=True
        )
        total = total + slope * product
    return -RELAX_RATE * total


def extend(field):
    layered = extended(field, (("rad", 1),), 1, False)
    beside_all = extended(layered, (("lon", 2),), 1, True)
    return jnp.pad(beside_all, ((0, 0), (0, 0), (0, 0), (1, 1)))


def cell_features(lon_index, lat_index, total_lon, total_lat):
    theta = math.pi * (lat_index.astype(jnp.float32) + 0.5) / total_lat
    phi = 2.0 * math.pi * lon_index.astype(jnp.float32) / total_lon
    upward = jnp.broadcast_to(jnp.cos(theta)[None, :], (phi.shape[0], theta.shape[0]))
    eastern = jnp.sin(theta)[None, :] * jnp.cos(phi)[:, None]
    northern = jnp.sin(theta)[None, :] * jnp.sin(phi)[:, None]
    return jnp.stack([upward, eastern, northern]).reshape(3, -1)


def site_features(cells, total_lon, total_lat):
    lon_index = cells // total_lat
    lat_index = cells % total_lat
    theta = math.pi * (lat_index.astype(jnp.float32) + 0.5) / total_lat
    phi = 2.0 * math.pi * lon_index.astype(jnp.float32) / total_lon
    return jnp.stack(
        [jnp.cos(theta), jnp.sin(theta) * jnp.cos(phi), jnp.sin(theta) * jnp.sin(phi)], axis=1
    )


def kernel(site_feats, cell_feats):
    cosine = (
        site_feats[:, 0:1] * cell_feats[0:1]
        + site_feats[:, 1:2] * cell_feats[1:2]
        + site_feats[:, 2:3] * cell_feats[2:3]
    )
    chord = 2.0 - 2.0 * cosine
    return 1.0 / (1.0 + chord / KERNEL_WIDTH) + 0.5 * jnp.cos(KERNEL_WAVE * chord)


def group_size(total_rows, unit, cells):
    blocks = total_rows // unit
    chosen = 1
    for candidate in range(1, 9):
        if blocks % candidate == 0 and candidate * unit * cells <= 1048576:
            chosen = candidate
    return chosen * unit


def predict_rows(feats, cell_feats, surface_flat, unit):
    size = group_size(feats.shape[0], unit, cell_feats.shape[1])
    blocks = feats.reshape(-1, size, 3)

    def one_block(block):
        weights = kernel(block, cell_feats)
        return jnp.einsum(
            "sm,cm->sc",
            weights,
            surface_flat,
            precision=lax.Precision.HIGHEST,
            preferred_element_type=jnp.float32,
        )

    return lax.map(one_block, blocks).reshape(-1, 3)


def body(
    logvisc, momentum, displacement, ice_history, load_steps, site_cells, observed, site_weight
):
    rad_rows = logvisc.shape[0]
    lon_cols = logvisc.shape[1]
    lat_cells = logvisc.shape[2]
    site_rows = site_cells.shape[0]
    total_rad = rad_rows * lax.axis_size("rad")
    total_lon = lon_cols * lax.axis_size("lon")
    lat_width = lat_cells // lax.axis_size("rad")
    scale = 1.0 / math.sqrt(total_lon * lat_cells)
    rad_global = lax.axis_index("rad") * rad_rows + jnp.arange(rad_rows)
    lon_global = lax.axis_index("lon") * lon_cols + jnp.arange(lon_cols)
    depth_weight = jnp.exp(4.0 * (rad_global.astype(jnp.float32) - (total_rad - 1)) / total_rad)
    top_row = (rad_global == total_rad - 1).astype(jnp.float32)[None, :, None, None]
    upward = (jnp.arange(3) == 0).astype(jnp.float32)[:, None, None, None]
    fluidity = jnp.exp(-logvisc)
    fluid_pad = extend(fluidity[None])
    state = displacement
    saved = []
    for level in range(RELAX):
        padded = extend(state)
        saved.append(padded)
        load = lax.dynamic_index_in_dim(ice_history, load_steps[level], 0, keepdims=False)
        state = (
            state
            + RELAX_RATE * apply_operator(padded, fluid_pad)
            - LOAD_FACTOR * upward * top_row * load[None, None]
        )
    column = jnp.sum(depth_weight[None, :, None, None] * state, axis=1)
    lat_start = lax.axis_index("rad") * lat_width
    lat_band = lat_start + jnp.arange(lat_width)
    whole_column = lax.psum(column, "rad")
    band = lax.dynamic_slice_in_dim(whole_column, lat_start, lat_width, 2)
    band_feats = cell_features(lon_global, lat_band, total_lon, lat_cells)
    own_feats = site_features(site_cells, total_lon, lat_cells)
    all_feats = lax.all_gather(own_feats, "lon", axis=0, tiled=True)
    band_flat = band.reshape(3, -1)
    partial_pred = lax.psum_scatter(
        predict_rows(all_feats, band_feats, band_flat, site_rows) * scale,
        "lon",
        scatter_dimension=0,
        tiled=True,
    )
    predicted = lax.psum(partial_pred, "rad").T
    weighted = site_weight * (predicted - observed)
    misfit = lax.psum(jnp.sum(weighted * weighted), "lon") / (3 * total_lon // lon_cols * site_rows)
    adjoint_cells = cell_features(lon_global, jnp.arange(lat_cells), total_lon, lat_cells)
    packet = jnp.concatenate([own_feats, (site_weight * weighted).T], axis=1)
    piece = lax.all_gather(packet, "lon", axis=0, tiled=True)
    size = group_size(piece.shape[0], site_rows, adjoint_cells.shape[1])
    blocks = piece.reshape(-1, size, 6)

    def add_block(running, block):
        weights = kernel(block[:, :3], adjoint_cells)
        return (
            running
            + jnp.einsum(
                "sc,sm->cm",
                block[:, 3:],
                weights,
                precision=lax.Precision.HIGHEST,
                preferred_element_type=jnp.float32,
            ),
            None,
        )

    running, unused = lax.scan(
        add_block, jnp.zeros((3, adjoint_cells.shape[1]), jnp.float32), blocks
    )
    surface_adjoint = (running * scale).reshape(3, lon_cols, lat_cells)
    adjoint = depth_weight[None, :, None, None] * surface_adjoint[:, None]
    gradient_fluid = jnp.zeros((1, rad_rows, lon_cols, lat_cells), jnp.float32)
    for level in range(RELAX - 1, -1, -1):
        adjoint_pad = extend(adjoint)
        gradient_fluid = gradient_fluid + fluid_gradient(saved[level], adjoint_pad, fluid_pad)
        if level > 0:
            adjoint = adjoint + RELAX_RATE * apply_operator(adjoint_pad, fluid_pad)
    gradient = -fluidity * gradient_fluid[0] + PRIOR_WEIGHT * logvisc
    half_momentum = momentum - 0.5 * gradient
    new_logvisc = logvisc + half_momentum
    return (new_logvisc, half_momentum, misfit.reshape(1))


def solution(mesh):
    return jax.shard_map(
        body,
        mesh=mesh,
        in_specs=(
            P("rad", "lon", None),
            P("rad", "lon", None),
            P(None, "rad", "lon", None),
            P(None, "lon", None),
            P(),
            P("lon"),
            P(None, "lon"),
            P(None, "lon"),
        ),
        out_specs=(P("rad", "lon", None), P("rad", "lon", None), P()),
        check_vma=False,
    )
```

profile of v0, /device:TPU:6, one launch (start us, length us, event | category | flops | bytes accessed | tf_op | source)
XLA Modules:
  0.0 1209.8 jit_solution(8901349295984895374)
XLA Ops:
  1.4 15.6 %collective-permute-start.3 = (f32[3,1,4,512]{3,2,1,0:T(4,128)S(1)}, f32[3,1,4,512]{3,2,1,0:T(4,128)S(1)}, u32[]{:S(2)}, u32[]{:S(2)}) collective-permute-start(f32[3,1,4,512]{3,2,1,0:T(4,128)S(1)} %get-tuple-element.153), channel_id=1, source_target_pairs={{0,1},{1,2},{2,3},{3,4},{4,5},{5,6},{6,7},{8,9},{9,10},{10,11},{11... | collective-permute-start | bytes 73736 | tf_op jit(solution)/shard_map/ppermute | solution.py:22
  19.1 14.9 %collective-permute-start.2 = (f32[1,1,4,512]{3,2,1,0:T(4,128)S(1)}, f32[1,1,4,512]{3,2,1,0:T(4,128)S(1)}, u32[]{:S(2)}, u32[]{:S(2)}) collective-permute-start(f32[1,1,4,512]{3,2,1,0:T(4,128)S(1)} %get-tuple-element.163), channel_id=1, source_target_pairs={{0,1},{1,2},{2,3},{3,4},{4,5},{5,6},{6,7},{8,9},{9,10},{10,11},{11... | collective-permute-start | bytes 24584 | tf_op jit(solution)/shard_map/ppermute | solution.py:22
  34.0 1.9 collective-permute-start
  44.2 6.1 collective-permute-done
  52.3 12.4 %collective-permute-start.4 = (f32[1,14,1,512]{3,2,1,0:T(1,128)S(1)}, f32[1,14,1,512]{3,2,1,0:T(1,128)S(1)}, u32[]{:S(2)}, u32[]{:S(2)}) collective-permute-start(f32[1,14,1,512]{3,2,1,0:T(1,128)S(1)} %get-tuple-element.160), channel_id=1, source_target_pairs={{8,0},{16,8},{24,16},{32,24},{40,32},{48,40},{56,48},{64,56},{72,6... | collective-permute-start | bytes 86024 | tf_op jit(solution)/shard_map/ppermute | solution.py:25
  66.9 12.4 %collective-permute-start.5 = (f32[3,14,1,512]{3,2,1,0:T(1,128)S(1)}, f32[3,14,1,512]{3,2,1,0:T(1,128)S(1)}, u32[]{:S(2)}, u32[]{:S(2)}) collective-permute-start(f32[3,14,1,512]{3,2,1,0:T(1,128)S(1)} %get-tuple-element.146), channel_id=1, source_target_pairs={{8,0},{16,8},{24,16},{32,24},{40,32},{48,40},{56,48},{64,56},{72,6... | collective-permute-start | bytes 258056 | tf_op jit(solution)/shard_map/ppermute | solution.py:25
  83.3 8.5 collective-permute-start.9
  93.8 112.6 %all-gather = f32[64,12,3]{1,2,0:T(4,128)S(1)} all-gather(f32[1,12,3]{1,2,0:T(4,128)S(1)} %maximum_bitcast_fusion.1), channel_id=1, replica_groups=mesh['lon'=64,'rad'=8] {'lon'}, dimensions={0}, use_global_device_ids=true | all-gather | bytes 9360 | tf_op jit(solution)/shard_map/all_gather | solution.py:175
  209.6 2.2 collective-permute-start.11
  211.8 12.0 collective-permute-start.10
  229.1 65.8 %psum.21 = f32[3,4,512]{2,1,0:T(4,128)S(1)} all-reduce(f32[3,4,512]{2,1,0:T(4,128)} %multiply_reduce_fusion.6), channel_id=1, replica_groups=mesh['lon'=64,'rad'=8] {'rad'}, use_global_device_ids=true, to_apply=%region_1.2 | all-reduce | flops 6144 | bytes 49152 | tf_op jit(solution)/shard_map/psum | solution.py:171
  295.6 11.0 while.21
  306.8 422.6 %all-reduce.5 = f32[768,3]{0,1:T(4,128)S(1)} all-reduce(f32[768,3]{0,1:T(4,128)S(1)} %mul.762), channel_id=2, replica_groups=mesh['lon'=64,'rad'=8] {'lon'}, use_global_device_ids=true, to_apply=%region_4.5.clone | all-reduce | flops 2304 | bytes 18432
  729.5 35.5 %psum.22 = f32[3,12]{1,0:T(4,128)S(1)} all-reduce(f32[3,12]{1,0:T(4,128)S(1)} %dynamic-slice_bitcast_fusion.2), channel_id=1, replica_groups=mesh['lon'=64,'rad'=8] {'rad'}, use_global_device_ids=true, to_apply=%region_5.6 | all-reduce | flops 36 | bytes 288 | tf_op jit(solution)/shard_map/psum | solution.py:183
  766.3 113.3 %all-gather.1 = f32[64,12,6]{1,2,0:T(8,128)S(1)} all-gather(f32[1,12,6]{1,2,0:T(8,128)S(1)} %maximum_bitcast_fusion), channel_id=1, replica_groups=mesh['lon'=64,'rad'=8] {'lon'}, dimensions={0}, use_global_device_ids=true | all-gather | bytes 18720 | tf_op jit(solution)/shard_map/all_gather | solution.py:188
  880.4 28.1 %while.22 = (s32[]{:T(128)}, f32[3,2048]{1,0:T(4,128)S(1)}, f32[8,96,6]{1,0,2:T(8,128)S(1)}, f32[3,2048]{1,0:T(4,128)S(1)}, s32[]{:T(128)}, /*index=5*/s32[]{:T(128)}) while((s32[]{:T(128)}, f32[3,2048]{1,0:T(4,128)S(1)}, f32[8,96,6]{1,0,2:T(8,128)S(1)}, f32[3,2048]{1,0:T(4,128)S(1)}, s32[]{:T(128)}, /*index=5*/s32[]{:T(128)}) %tuple.102), condition=%wide.region_7.8_spmd.clone, body=%wide.region_6.7_spmd.clone.sunk | while | flops 9646083 | bytes 146267 | solution.py:206
  880.5 3.4 convolution_add_fusion.2
  884.0 3.4 convolution_add_fusion.2
  887.5 3.4 convolution_add_fusion.2
  891.0 3.4 convolution_add_fusion.2
  894.5 3.4 convolution_add_fusion.2
  898.0 3.4 convolution_add_fusion.2
  901.6 3.4 convolution_add_fusion.2
  905.1 3.4 convolution_add_fusion.2
  909.4 12.8 %collective-permute-start.13 = (f32[3,1,4,512]{3,2,1,0:T(4,128)S(1)}, f32[3,1,4,512]{3,2,1,0:T(4,128)S(1)}, u32[]{:S(2)}, u32[]{:S(2)}) collective-permute-start(f32[3,1,4,512]{3,2,1,0:T(4,128)S(1)} %get-tuple-element.149), channel_id=1, source_target_pairs={{0,1},{1,2},{2,3},{3,4},{4,5},{5,6},{6,7},{8,9},{9,10},{10,11},{11... | collective-permute-start | bytes 73736 | tf_op jit(solution)/shard_map/ppermute | solution.py:22
  924.1 14.6 %collective-permute-done.12 = f32[3,1,4,512]{3,2,1,0:T(4,128)S(1)} collective-permute-done((f32[3,1,4,512]{3,2,1,0:T(4,128)S(1)}, f32[3,1,4,512]{3,2,1,0:T(4,128)S(1)}, u32[]{:S(2)}, u32[]{:S(2)}) %collective-permute-start.12) | collective-permute-done | bytes 24608 | tf_op jit(solution)/shard_map/ppermute | solution.py:25
  941.5 12.4 %collective-permute-start.14 = (f32[3,14,1,512]{3,2,1,0:T(1,128)}, f32[3,14,1,512]{3,2,1,0:T(1,128)}, u32[]{:S(2)}, u32[]{:S(2)}) collective-permute-start(f32[3,14,1,512]{3,2,1,0:T(1,128)} %get-tuple-element.142), channel_id=1, source_target_pairs={{8,0},{16,8},{24,16},{32,24},{40,32},{48,40},{56,48},{64,56},{72,6... | collective-permute-start | bytes 258056 | tf_op jit(solution)/shard_map/ppermute | solution.py:25
  953.8 210.9 %psum.23 = f32[]{:T(128)} all-reduce(f32[]{:T(128)} %get-tuple-element.169), channel_id=1, replica_groups=mesh['lon'=64,'rad'=8] {'lon'}, use_global_device_ids=true, to_apply=%region_21.22 | all-reduce | flops 1 | bytes 8 | tf_op jit(solution)/shard_map/psum | solution.py:185
  1169.1 1.9 collective-permute-start.17
  1171.1 3.9 collective-permute-start.16
  1175.9 11.7 collective-permute-done.16
  1189.7 12.5 %collective-permute-start.18 = (f32[3,14,1,512]{3,2,1,0:T(1,128)S(1)}, f32[3,14,1,512]{3,2,1,0:T(1,128)S(1)}, u32[]{:S(2)}, u32[]{:S(2)}) collective-permute-start(f32[3,14,1,512]{3,2,1,0:T(1,128)S(1)} %get-tuple-element.140), channel_id=1, source_target_pairs={{8,0},{16,8},{24,16},{32,24},{40,32},{48,40},{56,48},{64,56},{72,6... | collective-permute-start | bytes 258056 | tf_op jit(solution)/shard_map/ppermute | solution.py:25
  (299 shorter events, 57.3 us)
Async XLA Ops:
  1.4 63.3 %collective-permute-start.3 = (f32[3,1,4,512]{3,2,1,0:T(4,128)S(1)}, f32[3,1,4,512]{3,2,1,0:T(4,128)S(1)}, u32[]{:S(2)}, u32[]{:S(2)}) collective-permute-start(f32[3,1,4,512]{3,2,1,0:T(4,128)S(1)} %get-tuple-element.153), channel_id=1, source_target_pairs={{0,1},{1,2},{2,3},{3,4},{4,5},{5,6},{6,7},{8,9},{9,10},{10,11},{11... | collective-permute-start | bytes 73736 | tf_op jit(solution)/shard_map/ppermute | solution.py:22
  17.1 47.7 %collective-permute-start.1 = (f32[3,1,4,512]{3,2,1,0:T(4,128)S(1)}, f32[3,1,4,512]{3,2,1,0:T(4,128)S(1)}, u32[]{:S(2)}, u32[]{:S(2)}) collective-permute-start(f32[3,1,4,512]{3,2,1,0:T(4,128)S(1)} %get-tuple-element.154), channel_id=1, source_target_pairs={{1,0},{2,1},{3,2},{4,3},{5,4},{6,5},{7,6},{9,8},{10,9},{11,10},{12... | collective-permute-start | bytes 73736 | tf_op jit(solution)/shard_map/ppermute | solution.py:25
  19.1 45.6 %copy-start = (f32[3,12,4,512]{3,2,1,0:T(4,128)S(1)}, f32[3,12,4,512]{3,2,1,0:T(4,128)}, u32[]{:S(2)}) copy-start(f32[3,12,4,512]{3,2,1,0:T(4,128)} %param.14) | copy-start | bytes 884740
  19.1 25.1 %collective-permute-start.2 = (f32[1,1,4,512]{3,2,1,0:T(4,128)S(1)}, f32[1,1,4,512]{3,2,1,0:T(4,128)S(1)}, u32[]{:S(2)}, u32[]{:S(2)}) collective-permute-start(f32[1,1,4,512]{3,2,1,0:T(4,128)S(1)} %get-tuple-element.163), channel_id=1, source_target_pairs={{0,1},{1,2},{2,3},{3,4},{4,5},{5,6},{6,7},{8,9},{9,10},{10,11},{11... | collective-permute-start | bytes 24584 | tf_op jit(solution)/shard_map/ppermute | solution.py:22
  34.0 16.4 %collective-permute-start = (f32[1,1,4,512]{3,2,1,0:T(4,128)S(1)}, f32[1,1,4,512]{3,2,1,0:T(4,128)S(1)}, u32[]{:S(2)}, u32[]{:S(2)}) collective-permute-start(f32[1,1,4,512]{3,2,1,0:T(4,128)S(1)} %get-tuple-element.164), channel_id=1, source_target_pairs={{1,0},{2,1},{3,2},{4,3},{5,4},{6,5},{7,6},{9,8},{10,9},{11,10},{12... | collective-permute-start | bytes 24584 | tf_op jit(solution)/shard_map/ppermute | solution.py:25
  39.4 54.3 %copy-start.56 = (f32[12,1]{0,1:T(1,128)}, f32[12,1]{0,1:T(1,128)S(1)}, u32[]{:S(2)}) copy-start(f32[12,1]{0,1:T(1,128)S(1)} %get-tuple-element.121) | copy-start | bytes 148
  39.5 54.2 %copy-start.51 = (f32[12,1]{0,1:T(1,128)}, f32[12,1]{0,1:T(1,128)S(1)}, u32[]{:S(2)}) copy-start(f32[12,1]{0,1:T(1,128)S(1)} %get-tuple-element.123) | copy-start | bytes 148
  39.5 54.2 %copy-start.58 = (f32[12,1]{0,1:T(1,128)}, f32[12,1]{0,1:T(1,128)S(1)}, u32[]{:S(2)}) copy-start(f32[12,1]{0,1:T(1,128)S(1)} %multiply_bitcast_fusion.1) | copy-start | bytes 148
  40.3 42.0 %copy-start.46 = (f32[3,12]{1,0:T(4,128)}, f32[3,12]{1,0:T(4,128)S(1)}, u32[]{:S(2)}) copy-start(f32[3,12]{1,0:T(4,128)S(1)} %broadcast_multiply_fusion.3) | copy-start | bytes 436
  44.2 35.4 %copy-start.38 = (f32[1,1,4,512]{3,2,1,0:T(4,128)}, f32[1,1,4,512]{3,2,1,0:T(4,128)S(1)}, u32[]{:S(2)}) copy-start(f32[1,1,4,512]{3,2,1,0:T(4,128)S(1)} %collective-permute-done.2) | copy-start | bytes 24580
  50.4 29.3 %copy-start.40 = (f32[1,1,4,512]{3,2,1,0:T(4,128)}, f32[1,1,4,512]{3,2,1,0:T(4,128)S(1)}, u32[]{:S(2)}) copy-start(f32[1,1,4,512]{3,2,1,0:T(4,128)S(1)} %collective-permute-done) | copy-start | bytes 24580
  50.4 28.9 %collective-permute-start.6 = (f32[1,14,1,512]{3,2,1,0:T(1,128)S(1)}, f32[1,14,1,512]{3,2,1,0:T(1,128)S(1)}, u32[]{:S(2)}, u32[]{:S(2)}) collective-permute-start(f32[1,14,1,512]{3,2,1,0:T(1,128)S(1)} %get-tuple-element.159), channel_id=1, source_target_pairs={{0,8},{8,16},{16,24},{24,32},{32,40},{40,48},{48,56},{56,64},{64,7... | collective-permute-start | bytes 86024 | tf_op jit(solution)/shard_map/ppermute | solution.py:22
  52.3 26.9 %collective-permute-start.4 = (f32[1,14,1,512]{3,2,1,0:T(1,128)S(1)}, f32[1,14,1,512]{3,2,1,0:T(1,128)S(1)}, u32[]{:S(2)}, u32[]{:S(2)}) collective-permute-start(f32[1,14,1,512]{3,2,1,0:T(1,128)S(1)} %get-tuple-element.160), channel_id=1, source_target_pairs={{8,0},{16,8},{24,16},{32,24},{40,32},{48,40},{56,48},{64,56},{72,6... | collective-permute-start | bytes 86024 | tf_op jit(solution)/shard_map/ppermute | solution.py:25
  65.0 15.3 %collective-permute-start.7 = (f32[3,14,1,512]{3,2,1,0:T(1,128)S(1)}, f32[3,14,1,512]{3,2,1,0:T(1,128)S(1)}, u32[]{:S(2)}, u32[]{:S(2)}) collective-permute-start(f32[3,14,1,512]{3,2,1,0:T(1,128)S(1)} %get-tuple-element.145), channel_id=1, source_target_pairs={{0,8},{8,16},{16,24},{24,32},{32,40},{40,48},{48,56},{56,64},{64,7... | collective-permute-start | bytes 258056 | tf_op jit(solution)/shard_map/ppermute | solution.py:22
  66.9 14.6 %collective-permute-start.5 = (f32[3,14,1,512]{3,2,1,0:T(1,128)S(1)}, f32[3,14,1,512]{3,2,1,0:T(1,128)S(1)}, u32[]{:S(2)}, u32[]{:S(2)}) collective-permute-start(f32[3,14,1,512]{3,2,1,0:T(1,128)S(1)} %get-tuple-element.146), channel_id=1, source_target_pairs={{8,0},{16,8},{24,16},{32,24},{40,32},{48,40},{56,48},{64,56},{72,6... | collective-permute-start | bytes 258056 | tf_op jit(solution)/shard_map/ppermute | solution.py:25
  80.2 147.3 %copy-start.1 = (f32[12,4,512]{2,1,0:T(4,128)}, f32[12,4,512]{2,1,0:T(4,128)S(1)}, u32[]{:S(2)}) copy-start(f32[12,4,512]{2,1,0:T(4,128)S(1)} %get-tuple-element.157) | copy-start | bytes 294916
  80.2 147.3 %copy-start.3 = (f32[12,4,512]{2,1,0:T(4,128)}, f32[12,4,512]{2,1,0:T(4,128)S(1)}, u32[]{:S(2)}) copy-start(f32[12,4,512]{2,1,0:T(4,128)S(1)} %get-tuple-element.158) | copy-start | bytes 294916
  80.2 147.3 %copy-start.5 = (f32[12,4,512]{2,1,0:T(4,128)}, f32[12,4,512]{2,1,0:T(4,128)S(1)}, u32[]{:S(2)}) copy-start(f32[12,4,512]{2,1,0:T(4,128)S(1)} %get-tuple-element.161) | copy-start | bytes 294916
  83.3 125.6 %collective-permute-start.9 = (f32[3,1,4,512]{3,2,1,0:T(4,128)S(1)}, f32[3,1,4,512]{3,2,1,0:T(4,128)S(1)}, u32[]{:S(2)}, u32[]{:S(2)}) collective-permute-start(f32[3,1,4,512]{3,2,1,0:T(4,128)S(1)} %get-tuple-element.151), channel_id=1, source_target_pairs={{0,1},{1,2},{2,3},{3,4},{4,5},{5,6},{6,7},{8,9},{9,10},{10,11},{11... | collective-permute-start | bytes 73736 | tf_op jit(solution)/shard_map/ppermute | solution.py:22
  91.8 117.2 %collective-permute-start.8 = (f32[3,1,4,512]{3,2,1,0:T(4,128)S(1)}, f32[3,1,4,512]{3,2,1,0:T(4,128)S(1)}, u32[]{:S(2)}, u32[]{:S(2)}) collective-permute-start(f32[3,1,4,512]{3,2,1,0:T(4,128)S(1)} %get-tuple-element.152), channel_id=1, source_target_pairs={{1,0},{2,1},{3,2},{4,3},{5,4},{6,5},{7,6},{9,8},{10,9},{11,10},{12... | collective-permute-start | bytes 73736 | tf_op jit(solution)/shard_map/ppermute | solution.py:25
  209.6 14.5 %collective-permute-start.11 = (f32[3,14,1,512]{3,2,1,0:T(1,128)S(1)}, f32[3,14,1,512]{3,2,1,0:T(1,128)S(1)}, u32[]{:S(2)}, u32[]{:S(2)}) collective-permute-start(f32[3,14,1,512]{3,2,1,0:T(1,128)S(1)} %get-tuple-element.143), channel_id=1, source_target_pairs={{0,8},{8,16},{16,24},{24,32},{32,40},{40,48},{48,56},{56,64},{64,7... | collective-permute-start | bytes 258056 | tf_op jit(solution)/shard_map/ppermute | solution.py:22
  211.8 14.1 %collective-permute-start.10 = (f32[3,14,1,512]{3,2,1,0:T(1,128)S(1)}, f32[3,14,1,512]{3,2,1,0:T(1,128)S(1)}, u32[]{:S(2)}, u32[]{:S(2)}) collective-permute-start(f32[3,14,1,512]{3,2,1,0:T(1,128)S(1)} %get-tuple-element.144), channel_id=1, source_target_pairs={{8,0},{16,8},{24,16},{32,24},{40,32},{48,40},{56,48},{64,56},{72,6... | collective-permute-start | bytes 258056 | tf_op jit(solution)/shard_map/ppermute | solution.py:25
  729.5 35.5 %copy-start.53 = (f32[3,12]{1,0:T(4,128)S(1)}, f32[3,12]{1,0:T(4,128)}, u32[]{:S(2)}) copy-start(f32[3,12]{1,0:T(4,128)} %param.19) | copy-start | bytes 436
  729.5 35.5 %copy-start.54 = (f32[3,12]{1,0:T(4,128)S(1)}, f32[3,12]{1,0:T(4,128)}, u32[]{:S(2)}) copy-start(f32[3,12]{1,0:T(4,128)} %param.18) | copy-start | bytes 436
  909.4 14.7 %collective-permute-start.13 = (f32[3,1,4,512]{3,2,1,0:T(4,128)S(1)}, f32[3,1,4,512]{3,2,1,0:T(4,128)S(1)}, u32[]{:S(2)}, u32[]{:S(2)}) collective-permute-start(f32[3,1,4,512]{3,2,1,0:T(4,128)S(1)} %get-tuple-element.149), channel_id=1, source_target_pairs={{0,1},{1,2},{2,3},{3,4},{4,5},{5,6},{6,7},{8,9},{9,10},{10,11},{11... | collective-permute-start | bytes 73736 | tf_op jit(solution)/shard_map/ppermute | solution.py:22
  922.2 16.5 %collective-permute-start.12 = (f32[3,1,4,512]{3,2,1,0:T(4,128)S(1)}, f32[3,1,4,512]{3,2,1,0:T(4,128)S(1)}, u32[]{:S(2)}, u32[]{:S(2)}) collective-permute-start(f32[3,1,4,512]{3,2,1,0:T(4,128)S(1)} %get-tuple-element.150), channel_id=1, source_target_pairs={{1,0},{2,1},{3,2},{4,3},{5,4},{6,5},{7,6},{9,8},{10,9},{11,10},{12... | collective-permute-start | bytes 73736 | tf_op jit(solution)/shard_map/ppermute | solution.py:25
  939.5 225.9 %collective-permute-start.15 = (f32[3,14,1,512]{3,2,1,0:T(1,128)}, f32[3,14,1,512]{3,2,1,0:T(1,128)}, u32[]{:S(2)}, u32[]{:S(2)}) collective-permute-start(f32[3,14,1,512]{3,2,1,0:T(1,128)} %get-tuple-element.141), channel_id=1, source_target_pairs={{0,8},{8,16},{16,24},{24,32},{32,40},{40,48},{48,56},{56,64},{64,7... | collective-permute-start | bytes 258056 | tf_op jit(solution)/shard_map/ppermute | solution.py:22
  941.5 224.0 %collective-permute-start.14 = (f32[3,14,1,512]{3,2,1,0:T(1,128)}, f32[3,14,1,512]{3,2,1,0:T(1,128)}, u32[]{:S(2)}, u32[]{:S(2)}) collective-permute-start(f32[3,14,1,512]{3,2,1,0:T(1,128)} %get-tuple-element.142), channel_id=1, source_target_pairs={{8,0},{16,8},{24,16},{32,24},{40,32},{48,40},{56,48},{64,56},{72,6... | collective-permute-start | bytes 258056 | tf_op jit(solution)/shard_map/ppermute | solution.py:25
  1169.1 6.8 collective-permute-start.17
  1171.1 16.5 %collective-permute-start.16 = (f32[3,1,4,512]{3,2,1,0:T(4,128)S(1)}, f32[3,1,4,512]{3,2,1,0:T(4,128)S(1)}, u32[]{:S(2)}, u32[]{:S(2)}) collective-permute-start(f32[3,1,4,512]{3,2,1,0:T(4,128)S(1)} %get-tuple-element.148), channel_id=1, source_target_pairs={{1,0},{2,1},{3,2},{4,3},{5,4},{6,5},{7,6},{9,8},{10,9},{11,10},{12... | collective-permute-start | bytes 73736 | tf_op jit(solution)/shard_map/ppermute | solution.py:25
  1187.7 16.2 %collective-permute-start.19 = (f32[3,14,1,512]{3,2,1,0:T(1,128)S(1)}, f32[3,14,1,512]{3,2,1,0:T(1,128)S(1)}, u32[]{:S(2)}, u32[]{:S(2)}) collective-permute-start(f32[3,14,1,512]{3,2,1,0:T(1,128)S(1)} %get-tuple-element.139), channel_id=1, source_target_pairs={{0,8},{8,16},{16,24},{24,32},{32,40},{40,48},{48,56},{56,64},{64,7... | collective-permute-start | bytes 258056 | tf_op jit(solution)/shard_map/ppermute | solution.py:22
  1189.7 14.6 %collective-permute-start.18 = (f32[3,14,1,512]{3,2,1,0:T(1,128)S(1)}, f32[3,14,1,512]{3,2,1,0:T(1,128)S(1)}, u32[]{:S(2)}, u32[]{:S(2)}) collective-permute-start(f32[3,14,1,512]{3,2,1,0:T(1,128)S(1)} %get-tuple-element.140), channel_id=1, source_target_pairs={{8,0},{16,8},{24,16},{32,24},{40,32},{48,40},{56,48},{64,56},{72,6... | collective-permute-start | bytes 258056 | tf_op jit(solution)/shard_map/ppermute | solution.py:25
  (49 other events, 287.0 us)
where the time goes:
time: 1210 us
  blocking collectives  961 us (79%)
  starting transfers between devices  137 us (11%)
  waiting for transfers between devices  36.1 us (3%)
  matrix products  32.3 us (3%)
  other arithmetic  19.4 us (2%)
  local copies, waits for them, and re-layouts  16 us (1%)
    unnamed x1, blocking collectives  423 us
    psum x1, blocking collectives, body(): lax.psum(jnp.sum(weighted * weighted), 'lon')  211 us
    all_gather x1, blocking collectives, body(): piece = lax.all_gather(packet, 'lon', axis=0, tiled=True)  113 us
    all_gather x1, blocking collectives, body(): all_feats = lax.all_gather(own_feats, 'lon', axis=0, tiled=True)  113 us
    ppermute x10, starting transfers between devices, extended(): lax.ppermute(lax.slice_in_dim(block, 0, width, axis=dim), axis, backward)  73.2 us
    psum x1, blocking collectives, body(): whole_column = lax.psum(column, 'rad')  65.8 us
    ppermute x10, starting transfers between devices, extended(): lax.ppermute(lax.slice_in_dim(block, block.shape[dim] - width, None, axis...  63.6 us
    ppermute x10, waiting for transfers between devices, extended(): lax.ppermute(lax.slice_in_dim(block, 0, width, axis=dim), axis, backward)  35.9 us
  transfers between devices with their start and end apart: 20, of which 7 were waited for; matrix products, arithmetic and copies ran while one was open for 1% of the time, Pallas kernels for 0%

commit v1 on v0

--- a/solution.py
+++ b/solution.py
@@ -185,7 +185,9 @@
     misfit = lax.psum(jnp.sum(weighted * weighted), "lon") / (3 * total_lon // lon_cols * site_rows)
     adjoint_cells = cell_features(lon_global, jnp.arange(lat_cells), total_lon, lat_cells)
     packet = jnp.concatenate([own_feats, (site_weight * weighted).T], axis=1)
-    piece = lax.all_gather(packet, "lon", axis=0, tiled=True)
+    piece = jnp.concatenate(
+        lax.all_to_all(jnp.stack([packet] * lax.axis_size("lon")), "lon", 0, 0), axis=0
+    )
     size = group_size(piece.shape[0], site_rows, adjoint_cells.shape[1])
     blocks = piece.reshape(-1, size, 6)
 

time: 1210 us -> 1130 us (0.934)
  blocking collectives: 961 us -> 847 us
  waiting for transfers between devices: 36.1 us -> 56.1 us
    all_gather x1 -> x0, blocking collectives: 113 us -> none  [body(): piece = lax.all_gather(packet, 'lon', axis=0, tiled=True)]
    all_to_all x0 -> x1, waiting for transfers between devices: none -> 19.8 us  [body(): lax.all_to_all(jnp.stack([packet] * lax.axis_size('lon')), 'lon', 0, 0)]
  transfers between devices with their start and end apart: 20 -> 21, of which waited for: 7 -> 8; matrix products, arithmetic and copies ran while one was open for 1% -> 1% of each run, Pallas kernels for 0% -> 0%
where the time goes in v1:
time: 1130 us; the launch traced here: 1120 us
  blocking collectives  847 us (75%)
  starting transfers between devices  142 us (13%)
  waiting for transfers between devices  56.1 us (5%)
  matrix products  32.3 us (3%)
  other arithmetic  19.3 us (2%)
  local copies, waits for them, and re-layouts  18.4 us (2%)
    unnamed x1, blocking collectives  423 us
    psum x1, blocking collectives, body(): lax.psum(jnp.sum(weighted * weighted), 'lon')  211 us
    all_gather x1, blocking collectives, body(): all_feats = lax.all_gather(own_feats, 'lon', axis=0, tiled=True)  113 us
    ppermute x10, starting transfers between devices, extended(): lax.ppermute(lax.slice_in_dim(block, 0, width, axis=dim), axis, backward)  73.2 us
    psum x1, blocking collectives, body(): whole_column = lax.psum(column, 'rad')  65.8 us
    ppermute x10, starting transfers between devices, extended(): lax.ppermute(lax.slice_in_dim(block, block.shape[dim] - width, None, axis...  63.6 us
    ppermute x10, waiting for transfers between devices, extended(): lax.ppermute(lax.slice_in_dim(block, 0, width, axis=dim), axis, backward)  36.1 us
    psum x1, blocking collectives, body(): predicted = lax.psum(partial_pred, 'rad').T  35.4 us
  transfers between devices with their start and end apart: 21, of which 8 were waited for; matrix products, arithmetic and copies ran while one was open for 1% of the time, Pallas kernels for 0%

profile of v1, /device:TPU:6, one launch (start us, length us, event | category | flops | bytes accessed | tf_op | source)
XLA Modules:
  0.0 1123.7 jit_solution(9706725035716149146)
XLA Ops:
  1.4 15.6 %collective-permute-start.3 = (f32[3,1,4,512]{3,2,1,0:T(4,128)S(1)}, f32[3,1,4,512]{3,2,1,0:T(4,128)S(1)}, u32[]{:S(2)}, u32[]{:S(2)}) collective-permute-start(f32[3,1,4,512]{3,2,1,0:T(4,128)S(1)} %get-tuple-element.153), channel_id=1, source_target_pairs={{0,1},{1,2},{2,3},{3,4},{4,5},{5,6},{6,7},{8,9},{9,10},{10,11},{11... | collective-permute-start | bytes 73736 | tf_op jit(solution)/shard_map/ppermute | solution.py:22
  19.1 14.9 %collective-permute-start.2 = (f32[1,1,4,512]{3,2,1,0:T(4,128)S(1)}, f32[1,1,4,512]{3,2,1,0:T(4,128)S(1)}, u32[]{:S(2)}, u32[]{:S(2)}) collective-permute-start(f32[1,1,4,512]{3,2,1,0:T(4,128)S(1)} %get-tuple-element.163), channel_id=1, source_target_pairs={{0,1},{1,2},{2,3},{3,4},{4,5},{5,6},{6,7},{8,9},{9,10},{10,11},{11... | collective-permute-start | bytes 24584 | tf_op jit(solution)/shard_map/ppermute | solution.py:22
  34.0 1.9 collective-permute-start
  44.2 6.2 collective-permute-done
  52.3 12.4 %collective-permute-start.4 = (f32[1,14,1,512]{3,2,1,0:T(1,128)S(1)}, f32[1,14,1,512]{3,2,1,0:T(1,128)S(1)}, u32[]{:S(2)}, u32[]{:S(2)}) collective-permute-start(f32[1,14,1,512]{3,2,1,0:T(1,128)S(1)} %get-tuple-element.160), channel_id=1, source_target_pairs={{8,0},{16,8},{24,16},{32,24},{40,32},{48,40},{56,48},{64,56},{72,6... | collective-permute-start | bytes 86024 | tf_op jit(solution)/shard_map/ppermute | solution.py:25
  66.9 12.4 %collective-permute-start.5 = (f32[3,14,1,512]{3,2,1,0:T(1,128)S(1)}, f32[3,14,1,512]{3,2,1,0:T(1,128)S(1)}, u32[]{:S(2)}, u32[]{:S(2)}) collective-permute-start(f32[3,14,1,512]{3,2,1,0:T(1,128)S(1)} %get-tuple-element.146), channel_id=1, source_target_pairs={{8,0},{16,8},{24,16},{32,24},{40,32},{48,40},{56,48},{64,56},{72,6... | collective-permute-start | bytes 258056 | tf_op jit(solution)/shard_map/ppermute | solution.py:25
  83.3 8.4 collective-permute-start.9
  94.3 112.6 %all-gather = f32[64,12,3]{1,2,0:T(4,128)S(1)} all-gather(f32[1,12,3]{1,2,0:T(4,128)S(1)} %maximum_bitcast_fusion), channel_id=1, replica_groups=mesh['lon'=64,'rad'=8] {'lon'}, dimensions={0}, use_global_device_ids=true | all-gather | bytes 9360 | tf_op jit(solution)/shard_map/all_gather | solution.py:175
  210.3 2.2 collective-permute-start.11
  212.5 12.0 %collective-permute-start.10 = (f32[3,14,1,512]{3,2,1,0:T(1,128)S(1)}, f32[3,14,1,512]{3,2,1,0:T(1,128)S(1)}, u32[]{:S(2)}, u32[]{:S(2)}) collective-permute-start(f32[3,14,1,512]{3,2,1,0:T(1,128)S(1)} %get-tuple-element.144), channel_id=1, source_target_pairs={{8,0},{16,8},{24,16},{32,24},{40,32},{48,40},{56,48},{64,56},{72,6... | collective-permute-start | bytes 258056 | tf_op jit(solution)/shard_map/ppermute | solution.py:25
  229.8 65.8 %psum.21 = f32[3,4,512]{2,1,0:T(4,128)S(1)} all-reduce(f32[3,4,512]{2,1,0:T(4,128)} %multiply_reduce_fusion.6), channel_id=1, replica_groups=mesh['lon'=64,'rad'=8] {'rad'}, use_global_device_ids=true, to_apply=%region_1.2 | all-reduce | flops 6144 | bytes 49152 | tf_op jit(solution)/shard_map/psum | solution.py:171
  296.4 11.0 while.21
  307.5 422.7 %all-reduce.5 = f32[768,3]{0,1:T(4,128)S(1)} all-reduce(f32[768,3]{0,1:T(4,128)S(1)} %mul.762), channel_id=2, replica_groups=mesh['lon'=64,'rad'=8] {'lon'}, use_global_device_ids=true, to_apply=%region_4.5.clone | all-reduce | flops 2304 | bytes 18432
  730.2 35.4 %psum.22 = f32[3,12]{1,0:T(4,128)S(1)} all-reduce(f32[3,12]{1,0:T(4,128)S(1)} %dynamic-slice_bitcast_fusion.2), channel_id=1, replica_groups=mesh['lon'=64,'rad'=8] {'rad'}, use_global_device_ids=true, to_apply=%region_5.6 | all-reduce | flops 36 | bytes 288 | tf_op jit(solution)/shard_map/psum | solution.py:183
  767.7 4.9 all-to-all-start
  772.7 19.8 %all-to-all-done = f32[64,12,6]{1,2,0:T(8,128)S(1)} async-done(((f32[64,12,6]{1,2,0:T(8,128)}), f32[64,12,6]{1,2,0:T(8,128)S(1)}, u32[]{:S(2)}, u32[]{:S(2)}) %all-to-all-start) | async-done | bytes 18464 | tf_op jit(solution)/shard_map/all_to_all | solution.py:189
  794.3 28.2 %while.22 = (s32[]{:T(128)}, f32[3,2048]{1,0:T(4,128)S(1)}, f32[8,96,6]{1,0,2:T(8,128)S(1)}, f32[3,2048]{1,0:T(4,128)S(1)}, s32[]{:T(128)}, /*index=5*/s32[]{:T(128)}) while((s32[]{:T(128)}, f32[3,2048]{1,0:T(4,128)S(1)}, f32[8,96,6]{1,0,2:T(8,128)S(1)}, f32[3,2048]{1,0:T(4,128)S(1)}, s32[]{:T(128)}, /*index=5*/s32[]{:T(128)}) %tuple.101), condition=%wide.region_7.8_spmd.clone, body=%wide.region_6.7_spmd.clone.sunk | while | flops 9646083 | bytes 146267 | solution.py:208
  794.4 3.4 convolution_add_fusion.2
  797.9 3.4 convolution_add_fusion.2
  801.4 3.4 convolution_add_fusion.2
  804.9 3.4 convolution_add_fusion.2
  808.4 3.4 convolution_add_fusion.2
  812.0 3.4 convolution_add_fusion.2
  815.5 3.4 convolution_add_fusion.2
  819.0 3.4 convolution_add_fusion.2
  823.2 12.8 %collective-permute-start.13 = (f32[3,1,4,512]{3,2,1,0:T(4,128)S(1)}, f32[3,1,4,512]{3,2,1,0:T(4,128)S(1)}, u32[]{:S(2)}, u32[]{:S(2)}) collective-permute-start(f32[3,1,4,512]{3,2,1,0:T(4,128)S(1)} %get-tuple-element.149), channel_id=1, source_target_pairs={{0,1},{1,2},{2,3},{3,4},{4,5},{5,6},{6,7},{8,9},{9,10},{10,11},{11... | collective-permute-start | bytes 73736 | tf_op jit(solution)/shard_map/ppermute | solution.py:22
  838.0 14.7 %collective-permute-done.12 = f32[3,1,4,512]{3,2,1,0:T(4,128)S(1)} collective-permute-done((f32[3,1,4,512]{3,2,1,0:T(4,128)S(1)}, f32[3,1,4,512]{3,2,1,0:T(4,128)S(1)}, u32[]{:S(2)}, u32[]{:S(2)}) %collective-permute-start.12) | collective-permute-done | bytes 24608 | tf_op jit(solution)/shard_map/ppermute | solution.py:25
  855.4 12.4 %collective-permute-start.14 = (f32[3,14,1,512]{3,2,1,0:T(1,128)}, f32[3,14,1,512]{3,2,1,0:T(1,128)}, u32[]{:S(2)}, u32[]{:S(2)}) collective-permute-start(f32[3,14,1,512]{3,2,1,0:T(1,128)} %get-tuple-element.142), channel_id=1, source_target_pairs={{8,0},{16,8},{24,16},{32,24},{40,32},{48,40},{56,48},{64,56},{72,6... | collective-permute-start | bytes 258056 | tf_op jit(solution)/shard_map/ppermute | solution.py:25
  867.8 210.9 %psum.23 = f32[]{:T(128)} all-reduce(f32[]{:T(128)} %get-tuple-element.169), channel_id=1, replica_groups=mesh['lon'=64,'rad'=8] {'lon'}, use_global_device_ids=true, to_apply=%region_21.22 | all-reduce | flops 1 | bytes 8 | tf_op jit(solution)/shard_map/psum | solution.py:185
  1085.0 3.9 collective-permute-start.16
  1089.8 11.7 %collective-permute-done.16 = f32[3,1,4,512]{3,2,1,0:T(4,128)S(1)} collective-permute-done((f32[3,1,4,512]{3,2,1,0:T(4,128)S(1)}, f32[3,1,4,512]{3,2,1,0:T(4,128)S(1)}, u32[]{:S(2)}, u32[]{:S(2)}) %collective-permute-start.16) | collective-permute-done | bytes 24608 | tf_op jit(solution)/shard_map/ppermute | solution.py:25
  1103.6 12.5 %collective-permute-start.18 = (f32[3,14,1,512]{3,2,1,0:T(1,128)S(1)}, f32[3,14,1,512]{3,2,1,0:T(1,128)S(1)}, u32[]{:S(2)}, u32[]{:S(2)}) collective-permute-start(f32[3,14,1,512]{3,2,1,0:T(1,128)S(1)} %get-tuple-element.140), channel_id=1, source_target_pairs={{8,0},{16,8},{24,16},{32,24},{40,32},{48,40},{56,48},{64,56},{72,6... | collective-permute-start | bytes 258056 | tf_op jit(solution)/shard_map/ppermute | solution.py:25
  (305 shorter events, 61.5 us)
Async XLA Ops:
  1.4 63.3 %collective-permute-start.3 = (f32[3,1,4,512]{3,2,1,0:T(4,128)S(1)}, f32[3,1,4,512]{3,2,1,0:T(4,128)S(1)}, u32[]{:S(2)}, u32[]{:S(2)}) collective-permute-start(f32[3,1,4,512]{3,2,1,0:T(4,128)S(1)} %get-tuple-element.153), channel_id=1, source_target_pairs={{0,1},{1,2},{2,3},{3,4},{4,5},{5,6},{6,7},{8,9},{9,10},{10,11},{11... | collective-permute-start | bytes 73736 | tf_op jit(solution)/shard_map/ppermute | solution.py:22
  17.1 47.7 %collective-permute-start.1 = (f32[3,1,4,512]{3,2,1,0:T(4,128)S(1)}, f32[3,1,4,512]{3,2,1,0:T(4,128)S(1)}, u32[]{:S(2)}, u32[]{:S(2)}) collective-permute-start(f32[3,1,4,512]{3,2,1,0:T(4,128)S(1)} %get-tuple-element.154), channel_id=1, source_target_pairs={{1,0},{2,1},{3,2},{4,3},{5,4},{6,5},{7,6},{9,8},{10,9},{11,10},{12... | collective-permute-start | bytes 73736 | tf_op jit(solution)/shard_map/ppermute | solution.py:25
  19.1 45.7 %copy-start = (f32[3,12,4,512]{3,2,1,0:T(4,128)S(1)}, f32[3,12,4,512]{3,2,1,0:T(4,128)}, u32[]{:S(2)}) copy-start(f32[3,12,4,512]{3,2,1,0:T(4,128)} %param.14) | copy-start | bytes 884740
  19.1 25.1 %collective-permute-start.2 = (f32[1,1,4,512]{3,2,1,0:T(4,128)S(1)}, f32[1,1,4,512]{3,2,1,0:T(4,128)S(1)}, u32[]{:S(2)}, u32[]{:S(2)}) collective-permute-start(f32[1,1,4,512]{3,2,1,0:T(4,128)S(1)} %get-tuple-element.163), channel_id=1, source_target_pairs={{0,1},{1,2},{2,3},{3,4},{4,5},{5,6},{6,7},{8,9},{9,10},{10,11},{11... | collective-permute-start | bytes 24584 | tf_op jit(solution)/shard_map/ppermute | solution.py:22
  34.0 16.4 %collective-permute-start = (f32[1,1,4,512]{3,2,1,0:T(4,128)S(1)}, f32[1,1,4,512]{3,2,1,0:T(4,128)S(1)}, u32[]{:S(2)}, u32[]{:S(2)}) collective-permute-start(f32[1,1,4,512]{3,2,1,0:T(4,128)S(1)} %get-tuple-element.164), channel_id=1, source_target_pairs={{1,0},{2,1},{3,2},{4,3},{5,4},{6,5},{7,6},{9,8},{10,9},{11,10},{12... | collective-permute-start | bytes 24584 | tf_op jit(solution)/shard_map/ppermute | solution.py:25
  39.4 54.3 %copy-start.58 = (f32[12,1]{0,1:T(1,128)}, f32[12,1]{0,1:T(1,128)S(1)}, u32[]{:S(2)}) copy-start(f32[12,1]{0,1:T(1,128)S(1)} %get-tuple-element.121) | copy-start | bytes 148
  39.5 54.2 %copy-start.53 = (f32[12,1]{0,1:T(1,128)}, f32[12,1]{0,1:T(1,128)S(1)}, u32[]{:S(2)}) copy-start(f32[12,1]{0,1:T(1,128)S(1)} %get-tuple-element.123) | copy-start | bytes 148
  39.5 54.2 %copy-start.60 = (f32[12,1]{0,1:T(1,128)}, f32[12,1]{0,1:T(1,128)S(1)}, u32[]{:S(2)}) copy-start(f32[12,1]{0,1:T(1,128)S(1)} %multiply_bitcast_fusion.1) | copy-start | bytes 148
  40.3 42.0 %copy-start.48 = (f32[3,12]{1,0:T(4,128)}, f32[3,12]{1,0:T(4,128)S(1)}, u32[]{:S(2)}) copy-start(f32[3,12]{1,0:T(4,128)S(1)} %broadcast_multiply_fusion.3) | copy-start | bytes 436
  44.2 35.5 %copy-start.37 = (f32[1,1,4,512]{3,2,1,0:T(4,128)}, f32[1,1,4,512]{3,2,1,0:T(4,128)S(1)}, u32[]{:S(2)}) copy-start(f32[1,1,4,512]{3,2,1,0:T(4,128)S(1)} %collective-permute-done.2) | copy-start | bytes 24580
  50.4 28.9 %collective-permute-start.6 = (f32[1,14,1,512]{3,2,1,0:T(1,128)S(1)}, f32[1,14,1,512]{3,2,1,0:T(1,128)S(1)}, u32[]{:S(2)}, u32[]{:S(2)}) collective-permute-start(f32[1,14,1,512]{3,2,1,0:T(1,128)S(1)} %get-tuple-element.159), channel_id=1, source_target_pairs={{0,8},{8,16},{16,24},{24,32},{32,40},{40,48},{48,56},{56,64},{64,7... | collective-permute-start | bytes 86024 | tf_op jit(solution)/shard_map/ppermute | solution.py:22
  52.3 26.9 %collective-permute-start.4 = (f32[1,14,1,512]{3,2,1,0:T(1,128)S(1)}, f32[1,14,1,512]{3,2,1,0:T(1,128)S(1)}, u32[]{:S(2)}, u32[]{:S(2)}) collective-permute-start(f32[1,14,1,512]{3,2,1,0:T(1,128)S(1)} %get-tuple-element.160), channel_id=1, source_target_pairs={{8,0},{16,8},{24,16},{32,24},{40,32},{48,40},{56,48},{64,56},{72,6... | collective-permute-start | bytes 86024 | tf_op jit(solution)/shard_map/ppermute | solution.py:25
  65.0 15.3 %collective-permute-start.7 = (f32[3,14,1,512]{3,2,1,0:T(1,128)S(1)}, f32[3,14,1,512]{3,2,1,0:T(1,128)S(1)}, u32[]{:S(2)}, u32[]{:S(2)}) collective-permute-start(f32[3,14,1,512]{3,2,1,0:T(1,128)S(1)} %get-tuple-element.145), channel_id=1, source_target_pairs={{0,8},{8,16},{16,24},{24,32},{32,40},{40,48},{48,56},{56,64},{64,7... | collective-permute-start | bytes 258056 | tf_op jit(solution)/shard_map/ppermute | solution.py:22
  66.9 14.6 %collective-permute-start.5 = (f32[3,14,1,512]{3,2,1,0:T(1,128)S(1)}, f32[3,14,1,512]{3,2,1,0:T(1,128)S(1)}, u32[]{:S(2)}, u32[]{:S(2)}) collective-permute-start(f32[3,14,1,512]{3,2,1,0:T(1,128)S(1)} %get-tuple-element.146), channel_id=1, source_target_pairs={{8,0},{16,8},{24,16},{32,24},{40,32},{48,40},{56,48},{64,56},{72,6... | collective-permute-start | bytes 258056 | tf_op jit(solution)/shard_map/ppermute | solution.py:25
  80.2 148.0 %copy-start.1 = (f32[12,4,512]{2,1,0:T(4,128)}, f32[12,4,512]{2,1,0:T(4,128)S(1)}, u32[]{:S(2)}) copy-start(f32[12,4,512]{2,1,0:T(4,128)S(1)} %get-tuple-element.157) | copy-start | bytes 294916
  80.2 148.0 %copy-start.3 = (f32[12,4,512]{2,1,0:T(4,128)}, f32[12,4,512]{2,1,0:T(4,128)S(1)}, u32[]{:S(2)}) copy-start(f32[12,4,512]{2,1,0:T(4,128)S(1)} %get-tuple-element.158) | copy-start | bytes 294916
  80.2 148.0 %copy-start.5 = (f32[12,4,512]{2,1,0:T(4,128)}, f32[12,4,512]{2,1,0:T(4,128)S(1)}, u32[]{:S(2)}) copy-start(f32[12,4,512]{2,1,0:T(4,128)S(1)} %get-tuple-element.161) | copy-start | bytes 294916
  83.3 126.3 %collective-permute-start.9 = (f32[3,1,4,512]{3,2,1,0:T(4,128)S(1)}, f32[3,1,4,512]{3,2,1,0:T(4,128)S(1)}, u32[]{:S(2)}, u32[]{:S(2)}) collective-permute-start(f32[3,1,4,512]{3,2,1,0:T(4,128)S(1)} %get-tuple-element.151), channel_id=1, source_target_pairs={{0,1},{1,2},{2,3},{3,4},{4,5},{5,6},{6,7},{8,9},{9,10},{10,11},{11... | collective-permute-start | bytes 73736 | tf_op jit(solution)/shard_map/ppermute | solution.py:22
  91.7 117.9 %collective-permute-start.8 = (f32[3,1,4,512]{3,2,1,0:T(4,128)S(1)}, f32[3,1,4,512]{3,2,1,0:T(4,128)S(1)}, u32[]{:S(2)}, u32[]{:S(2)}) collective-permute-start(f32[3,1,4,512]{3,2,1,0:T(4,128)S(1)} %get-tuple-element.152), channel_id=1, source_target_pairs={{1,0},{2,1},{3,2},{4,3},{5,4},{6,5},{7,6},{9,8},{10,9},{11,10},{12... | collective-permute-start | bytes 73736 | tf_op jit(solution)/shard_map/ppermute | solution.py:25
  210.3 14.5 %collective-permute-start.11 = (f32[3,14,1,512]{3,2,1,0:T(1,128)S(1)}, f32[3,14,1,512]{3,2,1,0:T(1,128)S(1)}, u32[]{:S(2)}, u32[]{:S(2)}) collective-permute-start(f32[3,14,1,512]{3,2,1,0:T(1,128)S(1)} %get-tuple-element.143), channel_id=1, source_target_pairs={{0,8},{8,16},{16,24},{24,32},{32,40},{40,48},{48,56},{56,64},{64,7... | collective-permute-start | bytes 258056 | tf_op jit(solution)/shard_map/ppermute | solution.py:22
  212.5 14.1 %collective-permute-start.10 = (f32[3,14,1,512]{3,2,1,0:T(1,128)S(1)}, f32[3,14,1,512]{3,2,1,0:T(1,128)S(1)}, u32[]{:S(2)}, u32[]{:S(2)}) collective-permute-start(f32[3,14,1,512]{3,2,1,0:T(1,128)S(1)} %get-tuple-element.144), channel_id=1, source_target_pairs={{8,0},{16,8},{24,16},{32,24},{40,32},{48,40},{56,48},{64,56},{72,6... | collective-permute-start | bytes 258056 | tf_op jit(solution)/shard_map/ppermute | solution.py:25
  730.2 35.4 %copy-start.55 = (f32[3,12]{1,0:T(4,128)S(1)}, f32[3,12]{1,0:T(4,128)}, u32[]{:S(2)}) copy-start(f32[3,12]{1,0:T(4,128)} %param.19) | copy-start | bytes 436
  730.2 35.4 %copy-start.56 = (f32[3,12]{1,0:T(4,128)S(1)}, f32[3,12]{1,0:T(4,128)}, u32[]{:S(2)}) copy-start(f32[3,12]{1,0:T(4,128)} %param.18) | copy-start | bytes 436
  767.7 24.8 %all-to-all-start = ((f32[64,12,6]{1,2,0:T(8,128)}), f32[64,12,6]{1,2,0:T(8,128)S(1)}, u32[]{:S(2)}, u32[]{:S(2)}) async-start(f32[64,12,6]{1,2,0:T(8,128)} %stack.19), calls=%async_computation | async-start | bytes 524288 | tf_op jit(solution)/shard_map/all_to_all | solution.py:189
  823.2 14.8 %collective-permute-start.13 = (f32[3,1,4,512]{3,2,1,0:T(4,128)S(1)}, f32[3,1,4,512]{3,2,1,0:T(4,128)S(1)}, u32[]{:S(2)}, u32[]{:S(2)}) collective-permute-start(f32[3,1,4,512]{3,2,1,0:T(4,128)S(1)} %get-tuple-element.149), channel_id=1, source_target_pairs={{0,1},{1,2},{2,3},{3,4},{4,5},{5,6},{6,7},{8,9},{9,10},{10,11},{11... | collective-permute-start | bytes 73736 | tf_op jit(solution)/shard_map/ppermute | solution.py:22
  836.0 16.7 %collective-permute-start.12 = (f32[3,1,4,512]{3,2,1,0:T(4,128)S(1)}, f32[3,1,4,512]{3,2,1,0:T(4,128)S(1)}, u32[]{:S(2)}, u32[]{:S(2)}) collective-permute-start(f32[3,1,4,512]{3,2,1,0:T(4,128)S(1)} %get-tuple-element.150), channel_id=1, source_target_pairs={{1,0},{2,1},{3,2},{4,3},{5,4},{6,5},{7,6},{9,8},{10,9},{11,10},{12... | collective-permute-start | bytes 73736 | tf_op jit(solution)/shard_map/ppermute | solution.py:25
  853.5 225.9 %collective-permute-start.15 = (f32[3,14,1,512]{3,2,1,0:T(1,128)}, f32[3,14,1,512]{3,2,1,0:T(1,128)}, u32[]{:S(2)}, u32[]{:S(2)}) collective-permute-start(f32[3,14,1,512]{3,2,1,0:T(1,128)} %get-tuple-element.141), channel_id=1, source_target_pairs={{0,8},{8,16},{16,24},{24,32},{32,40},{40,48},{48,56},{56,64},{64,7... | collective-permute-start | bytes 258056 | tf_op jit(solution)/shard_map/ppermute | solution.py:22
  855.4 224.0 %collective-permute-start.14 = (f32[3,14,1,512]{3,2,1,0:T(1,128)}, f32[3,14,1,512]{3,2,1,0:T(1,128)}, u32[]{:S(2)}, u32[]{:S(2)}) collective-permute-start(f32[3,14,1,512]{3,2,1,0:T(1,128)} %get-tuple-element.142), channel_id=1, source_target_pairs={{8,0},{16,8},{24,16},{32,24},{40,32},{48,40},{56,48},{64,56},{72,6... | collective-permute-start | bytes 258056 | tf_op jit(solution)/shard_map/ppermute | solution.py:25
  1083.1 6.8 collective-permute-start.17
  1085.0 16.5 %collective-permute-start.16 = (f32[3,1,4,512]{3,2,1,0:T(4,128)S(1)}, f32[3,1,4,512]{3,2,1,0:T(4,128)S(1)}, u32[]{:S(2)}, u32[]{:S(2)}) collective-permute-start(f32[3,1,4,512]{3,2,1,0:T(4,128)S(1)} %get-tuple-element.148), channel_id=1, source_target_pairs={{1,0},{2,1},{3,2},{4,3},{5,4},{6,5},{7,6},{9,8},{10,9},{11,10},{12... | collective-permute-start | bytes 73736 | tf_op jit(solution)/shard_map/ppermute | solution.py:25
  1101.7 16.2 %collective-permute-start.19 = (f32[3,14,1,512]{3,2,1,0:T(1,128)S(1)}, f32[3,14,1,512]{3,2,1,0:T(1,128)S(1)}, u32[]{:S(2)}, u32[]{:S(2)}) collective-permute-start(f32[3,14,1,512]{3,2,1,0:T(1,128)S(1)} %get-tuple-element.139), channel_id=1, source_target_pairs={{0,8},{8,16},{16,24},{24,32},{32,40},{40,48},{48,56},{56,64},{64,7... | collective-permute-start | bytes 258056 | tf_op jit(solution)/shard_map/ppermute | solution.py:22
  1103.6 14.6 %collective-permute-start.18 = (f32[3,14,1,512]{3,2,1,0:T(1,128)S(1)}, f32[3,14,1,512]{3,2,1,0:T(1,128)S(1)}, u32[]{:S(2)}, u32[]{:S(2)}) collective-permute-start(f32[3,14,1,512]{3,2,1,0:T(1,128)S(1)} %get-tuple-element.140), channel_id=1, source_target_pairs={{8,0},{16,8},{24,16},{32,24},{40,32},{48,40},{56,48},{64,56},{72,6... | collective-permute-start | bytes 258056 | tf_op jit(solution)/shard_map/ppermute | solution.py:25
  (52 other events, 330.9 us)
